TPU v7x, 32 devices: a whole 2x2x4 slice. The times are simulated.
32 devices in a mesh: grp: 4 (over y, core), tile: 8 (over z, x).
Axes of the slice: x: 2, y: 2, z: 4, core: 2. Of those that a mesh axis runs over, the one named last changes fastest.
Arguments:
- adjoint_state: float32 [64, 128, 2048], P('tile', 'grp'), may hold values from -6 to 6
- misfit: float32 [64, 128, 2048], P('tile', 'grp'), may hold values from -4 to 4
- east_speed: float32 [64, 128, 2048], P('tile', 'grp'), may hold values from -0.6 to 0.6
- north_speed: float32 [64, 128, 2048], P('tile', 'grp'), may hold values from -0.6 to 0.6
- land_mask: int32 [64, 128, 2048], P('tile', 'grp'), may hold values 0 or 1
- warming_forcing_selector: int32 [128, 2048], P('grp', 'tile'), may hold values 0 or 1
- vertical_filter_matrix: float32 [64, 64], replicated, may hold values from 0 to 0.54
Outputs:
- filtered_thermal_sensitivity: float32 [64, 128, 2048], P('tile', 'grp')
- boundary_warming_sensitivity: float32 [128, 2048], P('grp', 'tile')
All inputs are finite; a program needn't handle non-finite values. No bound on the sum of `land_mask` or of `warming_forcing_selector` on one device may be relied on, other than what follows from the above.
Results may differ from a plain program's by a relative error of at most 0.000088.
Values sent between devices are 32-bit elements; how exact they have to be, the bound alone decides.
A program may use at most 192 MiB of HBM per device.

v0:
```python
import jax
import jax.numpy as jnp
from jax import lax
from jax.sharding import PartitionSpec as P

STEPS = 2


def with_halo(cells, sides, width):
    for axis, dim in sides:
        count = lax.axis_size(axis)
        ends = count - 1
        head = lax.slice_in_dim(cells, 0, width, axis=dim)
        tail = lax.slice_in_dim(cells, cells.shape[dim] - width, cells.shape[dim], axis=dim)
        cells = jnp.concatenate(
            [
                lax.ppermute(tail, axis, [(i, (i + 1) % count) for i in range(ends)]),
                cells,
                lax.ppermute(head, axis, [((i + 1) % count, i) for i in range(ends)]),
            ],
            axis=dim,
        )
    return cells


def advance(padded, misfit, east_speed, north_speed, wet_cells):
    center = padded[1:-1, 1:-1, 1:-1]
    east_cell = padded[1:-1, 1:-1, 2:]
    western_neighbour = padded[1:-1, 1:-1, :-2]
    north_cell = padded[1:-1, 2:, 1:-1]
    south_cell = padded[1:-1, :-2, 1:-1]
    upper_cell = padded[:-2, 1:-1, 1:-1]
    lower_cell = padded[2:, 1:-1, 1:-1]
    vertical = upper_cell + lower_cell - 2.0 * center
    lateral = east_cell + western_neighbour + north_cell + south_cell - 4.0 * center
    change = 0.5 * east_speed * (east_cell - western_neighbour) + 0.5 * north_speed * (
        north_cell - south_cell
    )
    return wet_cells * (center + misfit + change + 0.1 * lateral + 0.15 * vertical)


def smooth_levels(vertical_filter_matrix, pencil):
    return jnp.einsum(
        "cz,zne->cne", vertical_filter_matrix, pencil, precision=lax.Precision.HIGHEST
    )


def body(
    adjoint_state,
    misfit,
    east_speed,
    north_speed,
    land_mask,
    warming_forcing_selector,
    vertical_filter_matrix,
):
    wet_cells = land_mask.astype(jnp.float32)
    current_tracer_values = adjoint_state
    for step_index in range(STEPS):
        bordered = with_halo(current_tracer_values, (("grp", 1), ("tile", 0)), 1)
        padded = jnp.pad(bordered, ((0, 0), (0, 0), (1, 1)))
        current_tracer_values = advance(padded, misfit, east_speed, north_speed, wet_cells)
    pencil = lax.all_to_all(current_tracer_values, "tile", split_axis=2, concat_axis=0, tiled=True)
    smoothed_field = smooth_levels(vertical_filter_matrix, pencil)
    surface_layer = smoothed_field[0]
    filtered_thermal_sensitivity = lax.all_to_all(
        smoothed_field, "tile", split_axis=0, concat_axis=2, tiled=True
    )
    boundary_warming_sensitivity = warming_forcing_selector.astype(jnp.float32) * surface_layer
    return (filtered_thermal_sensitivity, boundary_warming_sensitivity)


def solution(mesh):
    in_specs = (
        P("tile", "grp", None),
        P("tile", "grp", None),
        P("tile", "grp", None),
        P("tile", "grp", None),
        P("tile", "grp", None),
        P("grp", "tile"),
        P(),
    )
    out_specs = (P("tile", "grp", None), P("grp", "tile"))
    return jax.shard_map(body, mesh=mesh, in_specs=in_specs, out_specs=out_specs, check_vma=False)
```

profile of v0, /device:TPU:0, one launch (start us, length us, event | category | flops | bytes accessed | tf_op | source)
XLA Modules:
  0.0 217.6 jit_solution(6359021577452492257)
XLA Ops:
  0.7 1.4 fusion.18
  2.1 2.4 %collective-permute-start = (f32[8,1,2048]{2,0,1:T(8,128)S(1)}, f32[8,1,2048]{2,0,1:T(8,128)S(1)}, u32[]{:S(2)}, u32[]{:S(2)}) collective-permute-start(f32[8,1,2048]{2,0,1:T(8,128)S(1)} %copy.101), channel_id=1, source_target_pairs={{0,8},{8,16},{16,24},{1,9},{9,17},{17,25},{2,10},{10,18},{18,26},{... | collective-permute-start | bytes 196616 | tf_op jit(solution)/shard_map/ppermute | solution.py:17
  4.5 1.3 collective-permute-start.1
  5.9 3.9 %collective-permute-done.1 = f32[8,1,2048]{2,0,1:T(8,128)S(1)} collective-permute-done((f32[8,1,2048]{2,0,1:T(8,128)S(1)}, f32[8,1,2048]{2,0,1:T(8,128)S(1)}, u32[]{:S(2)}, u32[]{:S(2)}) %collective-permute-start.1) | collective-permute-done | bytes 65568 | tf_op jit(solution)/shard_map/ppermute | solution.py:19
  9.9 1.1 pad_maximum_fusion.21
  11.0 3.4 %collective-permute-start.2 = (f32[1,34,2048]{2,1,0:T(8,128)S(1)}, f32[1,34,2048]{2,1,0:T(8,128)S(1)}, u32[]{:S(2)}, u32[]{:S(2)}) collective-permute-start(f32[1,34,2048]{2,1,0:T(8,128)S(1)} %get-tuple-element.4), channel_id=1, source_target_pairs={{0,1},{1,2},{2,3},{3,4},{4,5},{5,6},{6,7},{8,9},{9,10},{10,11},{11... | collective-permute-start | bytes 835592 | tf_op jit(solution)/shard_map/ppermute | solution.py:17
  14.5 1.6 collective-permute-start.3
  16.0 4.3 %collective-permute-done.2 = f32[1,34,2048]{2,1,0:T(8,128)S(1)} collective-permute-done((f32[1,34,2048]{2,1,0:T(8,128)S(1)}, f32[1,34,2048]{2,1,0:T(8,128)S(1)}, u32[]{:S(2)}, u32[]{:S(2)}) %collective-permute-start.2) | collective-permute-done | bytes 278560 | tf_op jit(solution)/shard_map/ppermute | solution.py:17
  20.3 5.0 %collective-permute-done.3 = f32[1,34,2048]{2,1,0:T(8,128)S(1)} collective-permute-done((f32[1,34,2048]{2,1,0:T(8,128)S(1)}, f32[1,34,2048]{2,1,0:T(8,128)S(1)}, u32[]{:S(2)}, u32[]{:S(2)}) %collective-permute-start.3) | collective-permute-done | bytes 278560 | tf_op jit(solution)/shard_map/ppermute | solution.py:19
  25.3 3.1 %select_maximum_fusion.4 = f32[10,34,2050]{2,1,0:T(8,128)S(1)} fusion(f32[1,34,2048]{2,1,0:T(8,128)S(1)} %collective-permute-done.3, f32[1,34,2048]{2,1,0:T(8,128)S(1)} %collective-permute-done.2, f32[8,1,2048]{2,1,0:T(1,128)S(1)} %copy.87, f32[8,32,2048]{2,1,0:T(8,128)S(1)} %copy-done.1, f32[8,1,2048]{2,1,0:T(1,128)S(1)} %copy.86), kind=kLoop, calls=%fused_computation.6 | loop fusion | flops 8364000 | bytes 5573280 | tf_op jit(solution)/shard_map/concatenate | solution.py:15
  28.5 4.3 %fusion.10 = f32[8,32,2048]{2,1,0:T(8,128)S(1)} fusion(f32[1,34,2048]{2,1,0:T(8,128)S(1)} %collective-permute-done.3, f32[8,1,2048]{2,1,0:T(1,128)S(1)} %copy.87, f32[8,32,2048]{2,1,0:T(8,128)S(1)} %copy-done.1, f32[8,1,2048]{2,1,0:T(1,128)S(1)} %copy.86, f32[1,34,2048]{2,1,0:T(8,128)S(1)} %collective-permute-done.2, ...), kind=kLoop, calls=%fused_computation.29 | loop fusion | flops 16252928 | bytes 17465344 | tf_op jit(solution)/shard_map/mul | solution.py:39
  32.9 6.2 %collective-permute-start.4 = (f32[8,1,2048]{2,0,1:T(8,128)S(1)}, f32[8,1,2048]{2,0,1:T(8,128)S(1)}, u32[]{:S(2)}, u32[]{:S(2)}) collective-permute-start(f32[8,1,2048]{2,0,1:T(8,128)S(1)} %copy.90), channel_id=1, source_target_pairs={{0,8},{8,16},{16,24},{1,9},{9,17},{17,25},{2,10},{10,18},{18,26},{... | collective-permute-start | bytes 196616 | tf_op jit(solution)/shard_map/ppermute | solution.py:17
  39.1 1.3 collective-permute-start.5
  40.5 1.8 collective-permute-done.5
  42.5 4.1 %collective-permute-start.6 = (f32[1,34,2048]{2,1,0:T(8,128)S(1)}, f32[1,34,2048]{2,1,0:T(8,128)S(1)}, u32[]{:S(2)}, u32[]{:S(2)}) collective-permute-start(f32[1,34,2048]{2,1,0:T(8,128)S(1)} %get-tuple-element.2), channel_id=1, source_target_pairs={{0,1},{1,2},{2,3},{3,4},{4,5},{5,6},{6,7},{8,9},{9,10},{10,11},{11... | collective-permute-start | bytes 835592 | tf_op jit(solution)/shard_map/ppermute | solution.py:17
  46.6 1.4 collective-permute-start.7
  48.0 5.1 %collective-permute-done.6 = f32[1,34,2048]{2,1,0:T(8,128)S(1)} collective-permute-done((f32[1,34,2048]{2,1,0:T(8,128)S(1)}, f32[1,34,2048]{2,1,0:T(8,128)S(1)}, u32[]{:S(2)}, u32[]{:S(2)}) %collective-permute-start.6) | collective-permute-done | bytes 278560 | tf_op jit(solution)/shard_map/ppermute | solution.py:17
  53.1 5.2 %collective-permute-done.7 = f32[1,34,2048]{2,1,0:T(8,128)S(1)} collective-permute-done((f32[1,34,2048]{2,1,0:T(8,128)S(1)}, f32[1,34,2048]{2,1,0:T(8,128)S(1)}, u32[]{:S(2)}, u32[]{:S(2)}) %collective-permute-start.7) | collective-permute-done | bytes 278560 | tf_op jit(solution)/shard_map/ppermute | solution.py:19
  58.3 3.1 %select_maximum_fusion = f32[10,34,2050]{2,1,0:T(8,128)S(1)} fusion(f32[1,34,2048]{2,1,0:T(8,128)S(1)} %collective-permute-done.7, f32[1,34,2048]{2,1,0:T(8,128)S(1)} %collective-permute-done.6, f32[8,1,2048]{2,1,0:T(1,128)S(1)} %copy.93, f32[8,32,2048]{2,1,0:T(8,128)S(1)} %fusion.10, f32[8,1,2048]{2,1,0:T(1,128)S(1)} %copy.92), kind=kLoop, calls=%fused_computation.2 | loop fusion | flops 8364000 | bytes 5573280 | tf_op jit(solution)/shard_map/concatenate | solution.py:15
  61.4 3.0 %fusion.5 = f32[8,32,2048]{2,1,0:T(8,128)S(1)} fusion(f32[1,34,2048]{2,1,0:T(8,128)S(1)} %collective-permute-done.7, f32[8,1,2048]{2,1,0:T(1,128)S(1)} %copy.93, f32[8,32,2048]{2,1,0:T(8,128)S(1)} %fusion.10, f32[8,1,2048]{2,1,0:T(1,128)S(1)} %copy.92, f32[1,34,2048]{2,1,0:T(8,128)S(1)} %collective-permute-done.6, ...), kind=kLoop, calls=%fused_computation.16 | loop fusion | flops 16252928 | bytes 17465344 | tf_op jit(solution)/shard_map/mul | solution.py:39
  64.5 4.7 %copy.96 = f32[8,32,2048]{1,0,2:T(8,128)} copy(f32[8,32,2048]{2,1,0:T(8,128)S(1)} %fusion.5) | data formatting | bytes 4194304 | tf_op jit(solution)/shard_map/mul | solution.py:39
  69.2 7.4 %reshape.5 = f32[8,1,65536]{2,1,0:T(1,128)S(1)} reshape(f32[2048,8,32]{2,1,0:T(8,128)} %bitcast.22) | data formatting | bytes 4194304
  76.6 59.5 %all_to_all.36 = f32[8,1,65536]{2,1,0:T(1,128)} all-to-all(f32[8,1,65536]{2,1,0:T(1,128)S(1)} %reshape.5), channel_id=1, replica_groups=mesh['grp'=4,'tile'=8] {'tile'}, dimensions={0} | all-to-all | bytes 4194304 | tf_op jit(solution)/shard_map/all_to_all | solution.py:63
  136.7 7.2 %reduce = f32[8,65536]{1,0:T(8,128)S(1)} reduce(f32[8,1,65536]{2,1,0:T(1,128)} %all_to_all.36, f32[]{:T(128)} %broadcast.70), dimensions={1}, to_apply=%all_to_all.26.reduce_sub_computation | reduce | bytes 4194308 | tf_op jit(solution)/shard_map/all_to_all | solution.py:63
  143.9 6.0 %reshape.6 = f32[2048,8,32]{2,1,0:T(8,128)} reshape(f32[8,65536]{1,0:T(8,128)S(1)} %reduce) | data formatting | bytes 4194304
  149.9 6.6 %copy.97 = f32[8,32,8,256]{3,0,2,1:T(8,128)} copy(f32[8,32,8,256]{1,0,3,2:T(8,128)} %bitcast.23) | data formatting | bytes 4194304 | tf_op jit(solution)/shard_map/all_to_all | solution.py:63
  156.5 3.6 %fusion.13 = f32[64,32,256]{2,0,1:T(8,128)S(1)} fusion(f32[8,32,8,256]{3,0,2,1:T(8,128)} %copy.97, f32[64,64]{1,0:T(8,128)S(1)} %copy-done), kind=kOutput, calls=%fused_computation.39 | convolution fusion | flops 402653184 | bytes 4210688 | tf_op jit(solution)/shard_map/cz,zne->cne/dot_general | solution.py:43
  160.1 2.5 %copy.98 = f32[64,32,256]{2,1,0:T(8,128)} copy(f32[64,32,256]{2,0,1:T(8,128)S(1)} %fusion.13) | data formatting | bytes 4194304 | tf_op jit(solution)/shard_map/cz,zne->cne/dot_general | solution.py:43
  162.6 4.5 %all-to-all-start.1 = ((f32[64,32,256]{2,1,0:T(8,128)}), f32[64,32,256]{2,1,0:T(8,128)}, u32[]{:S(2)}, u32[]{:S(2)}) async-start(f32[64,32,256]{2,1,0:T(8,128)} %copy.98), calls=%async_computation.1 | async-start | bytes 4194304 | tf_op jit(solution)/shard_map/all_to_all | solution.py:66
  167.1 0.6 bitcast_multiply_fusion
  167.8 46.7 %all-to-all-done.1 = f32[64,32,256]{2,1,0:T(8,128)} async-done(((f32[64,32,256]{2,1,0:T(8,128)}), f32[64,32,256]{2,1,0:T(8,128)}, u32[]{:S(2)}, u32[]{:S(2)}) %all-to-all-start.1) | async-done | bytes 2097184 | tf_op jit(solution)/shard_map/all_to_all | solution.py:66
  214.4 3.2 %copy.103 = f32[8,8,4,8,256]{4,3,0,2,1:T(8,128)} copy(f32[8,8,4,8,256]{4,3,2,1,0:T(8,128)} %bitcast.10) | data formatting | bytes 4194304 | tf_op jit(solution)/shard_map/all_to_all | solution.py:66
  (28 shorter events, 1.1 us)
Async XLA Ops:
  0.6 155.8 %copy-start = (f32[64,64]{1,0:T(8,128)S(1)}, f32[64,64]{1,0:T(8,128)}, u32[]{:S(2)}) copy-start(f32[64,64]{1,0:T(8,128)} %param.13) | copy-start | bytes 49156
  0.6 24.7 %copy-start.1 = (f32[8,32,2048]{2,1,0:T(8,128)S(1)}, f32[8,32,2048]{2,1,0:T(8,128)}, u32[]{:S(2)}) copy-start(f32[8,32,2048]{2,1,0:T(8,128)} %param.7) | copy-start | bytes 6291460
  2.1 3.7 %collective-permute-start = (f32[8,1,2048]{2,0,1:T(8,128)S(1)}, f32[8,1,2048]{2,0,1:T(8,128)S(1)}, u32[]{:S(2)}, u32[]{:S(2)}) collective-permute-start(f32[8,1,2048]{2,0,1:T(8,128)S(1)} %copy.101), channel_id=1, source_target_pairs={{0,8},{8,16},{16,24},{1,9},{9,17},{17,25},{2,10},{10,18},{18,26},{... | collective-permute-start | bytes 196616 | tf_op jit(solution)/shard_map/ppermute | solution.py:17
  4.5 5.3 %collective-permute-start.1 = (f32[8,1,2048]{2,0,1:T(8,128)S(1)}, f32[8,1,2048]{2,0,1:T(8,128)S(1)}, u32[]{:S(2)}, u32[]{:S(2)}) collective-permute-start(f32[8,1,2048]{2,0,1:T(8,128)S(1)} %copy.102), channel_id=1, source_target_pairs={{8,0},{16,8},{24,16},{9,1},{17,9},{25,17},{10,2},{18,10},{26,18},{... | collective-permute-start | bytes 196616 | tf_op jit(solution)/shard_map/ppermute | solution.py:19
  11.0 9.3 %collective-permute-start.2 = (f32[1,34,2048]{2,1,0:T(8,128)S(1)}, f32[1,34,2048]{2,1,0:T(8,128)S(1)}, u32[]{:S(2)}, u32[]{:S(2)}) collective-permute-start(f32[1,34,2048]{2,1,0:T(8,128)S(1)} %get-tuple-element.4), channel_id=1, source_target_pairs={{0,1},{1,2},{2,3},{3,4},{4,5},{5,6},{6,7},{8,9},{9,10},{10,11},{11... | collective-permute-start | bytes 835592 | tf_op jit(solution)/shard_map/ppermute | solution.py:17
  14.4 14.0 %copy-start.2 = (f32[8,32,2048]{2,1,0:T(8,128)S(1)}, f32[8,32,2048]{2,1,0:T(8,128)}, u32[]{:S(2)}) copy-start(f32[8,32,2048]{2,1,0:T(8,128)} %param.8) | copy-start | bytes 6291460
  14.4 14.0 %copy-start.3 = (s32[8,32,2048]{2,1,0:T(8,128)S(1)}, s32[8,32,2048]{2,1,0:T(8,128)}, u32[]{:S(2)}) copy-start(s32[8,32,2048]{2,1,0:T(8,128)} %param.11) | copy-start | bytes 6291460
  14.5 14.0 %copy-start.4 = (f32[8,32,2048]{2,1,0:T(8,128)S(1)}, f32[8,32,2048]{2,1,0:T(8,128)}, u32[]{:S(2)}) copy-start(f32[8,32,2048]{2,1,0:T(8,128)} %param.10) | copy-start | bytes 6291460
  14.5 10.9 %collective-permute-start.3 = (f32[1,34,2048]{2,1,0:T(8,128)S(1)}, f32[1,34,2048]{2,1,0:T(8,128)S(1)}, u32[]{:S(2)}, u32[]{:S(2)}) collective-permute-start(f32[1,34,2048]{2,1,0:T(8,128)S(1)} %get-tuple-element.5), channel_id=1, source_target_pairs={{1,0},{2,1},{3,2},{4,3},{5,4},{6,5},{7,6},{9,8},{10,9},{11,10},{12... | collective-permute-start | bytes 835592 | tf_op jit(solution)/shard_map/ppermute | solution.py:19
  32.9 7.6 %collective-permute-start.4 = (f32[8,1,2048]{2,0,1:T(8,128)S(1)}, f32[8,1,2048]{2,0,1:T(8,128)S(1)}, u32[]{:S(2)}, u32[]{:S(2)}) collective-permute-start(f32[8,1,2048]{2,0,1:T(8,128)S(1)} %copy.90), channel_id=1, source_target_pairs={{0,8},{8,16},{16,24},{1,9},{9,17},{17,25},{2,10},{10,18},{18,26},{... | collective-permute-start | bytes 196616 | tf_op jit(solution)/shard_map/ppermute | solution.py:17
  39.1 3.1 %collective-permute-start.5 = (f32[8,1,2048]{2,0,1:T(8,128)S(1)}, f32[8,1,2048]{2,0,1:T(8,128)S(1)}, u32[]{:S(2)}, u32[]{:S(2)}) collective-permute-start(f32[8,1,2048]{2,0,1:T(8,128)S(1)} %copy.91), channel_id=1, source_target_pairs={{8,0},{16,8},{24,16},{9,1},{17,9},{25,17},{10,2},{18,10},{26,18},{... | collective-permute-start | bytes 196616 | tf_op jit(solution)/shard_map/ppermute | solution.py:19
  42.5 10.6 %collective-permute-start.6 = (f32[1,34,2048]{2,1,0:T(8,128)S(1)}, f32[1,34,2048]{2,1,0:T(8,128)S(1)}, u32[]{:S(2)}, u32[]{:S(2)}) collective-permute-start(f32[1,34,2048]{2,1,0:T(8,128)S(1)} %get-tuple-element.2), channel_id=1, source_target_pairs={{0,1},{1,2},{2,3},{3,4},{4,5},{5,6},{6,7},{8,9},{9,10},{10,11},{11... | collective-permute-start | bytes 835592 | tf_op jit(solution)/shard_map/ppermute | solution.py:17
  46.6 14.8 %copy-start.5 = (f32[8,32,2048]{2,1,0:T(8,128)S(1)}, f32[8,32,2048]{2,1,0:T(8,128)}, u32[]{:S(2)}) copy-start(f32[8,32,2048]{2,1,0:T(8,128)} %param.9) | copy-start | bytes 6291460
  46.6 11.7 %collective-permute-start.7 = (f32[1,34,2048]{2,1,0:T(8,128)S(1)}, f32[1,34,2048]{2,1,0:T(8,128)S(1)}, u32[]{:S(2)}, u32[]{:S(2)}) collective-permute-start(f32[1,34,2048]{2,1,0:T(8,128)S(1)} %get-tuple-element.3), channel_id=1, source_target_pairs={{1,0},{2,1},{3,2},{4,3},{5,4},{6,5},{7,6},{9,8},{10,9},{11,10},{12... | collective-permute-start | bytes 835592 | tf_op jit(solution)/shard_map/ppermute | solution.py:19
  162.6 4.5 %copy-start.6 = (s32[32,256]{1,0:T(8,128)S(1)}, s32[32,256]{1,0:T(8,128)}, u32[]{:S(2)}) copy-start(s32[32,256]{1,0:T(8,128)} %param.12) | copy-start | bytes 98308
  162.6 51.8 %all-to-all-start.1 = ((f32[64,32,256]{2,1,0:T(8,128)}), f32[64,32,256]{2,1,0:T(8,128)}, u32[]{:S(2)}, u32[]{:S(2)}) async-start(f32[64,32,256]{2,1,0:T(8,128)} %copy.98), calls=%async_computation.1 | async-start | bytes 4194304 | tf_op jit(solution)/shard_map/all_to_all | solution.py:66
where the time goes:
time: 218 us
  waiting for transfers between devices  71.9 us (33%)
  blocking collectives  59.5 us (27%)
  local copies, waits for them, and re-layouts  32.9 us (15%)
  starting transfers between devices  26.2 us (12%)
  other arithmetic  22.6 us (10%)
  matrix products  3.6 us (2%)
    all_to_all x1, blocking collectives, body(): lax.all_to_all(current_tracer_values, 'tile', split_axis=2, concat_axis=0...  59.5 us
    all_to_all x1, waiting for transfers between devices, body(): lax.all_to_all(smoothed_field, 'tile', split_axis=0, concat_axis=2, tiled...  46.7 us
    ppermute x4, starting transfers between devices, with_halo(): lax.ppermute(tail, axis, [(i, (i + 1) % count) for i in range(ends)])  16.1 us
    ppermute x4, waiting for transfers between devices, with_halo(): lax.ppermute(head, axis, [((i + 1) % count, i) for i in range(ends)])  15.8 us
    unnamed x18, local copies, waits for them, and re-layouts  13.5 us
    ppermute x4, waiting for transfers between devices, with_halo(): lax.ppermute(tail, axis, [(i, (i + 1) % count) for i in range(ends)])  9.4 us
    mul x2, other arithmetic, advance(): wet_cells * (center + misfit + change + 0.1 * lateral + 0.15 * vertical)  7.31 us
    all_to_all x1, other arithmetic, body(): lax.all_to_all(current_tracer_values, 'tile', split_axis=2, concat_axis=0...  7.22 us
  transfers between devices with their start and end apart: 9, of which 7 were waited for; matrix products, arithmetic and copies ran while one was open for 0% of the time, Pallas kernels for 0%

commit v1 on v0

--- a/solution.py
+++ b/solution.py
@@ -4,6 +4,22 @@
 from jax.sharding import PartitionSpec as P
 
 STEPS = 2
+
+
+def pairwise_exchange(x, axis, split, join):
+    ways, here = (lax.axis_size(axis), lax.axis_index(axis))
+    width = x.shape[split] // ways
+    lengths = list(x.shape)
+    lengths[split] = width
+    height = lengths[join]
+    lengths[join] = height * ways
+    full = jnp.zeros(lengths, x.dtype)
+    for mask in range(ways):
+        part = lax.dynamic_slice_in_dim(x, (here ^ mask) * width, width, axis=split)
+        if mask:
+            part = lax.ppermute(part, axis, [(d, d ^ mask) for d in range(ways)])
+        full = lax.dynamic_update_slice_in_dim(full, part, (here ^ mask) * height, axis=join)
+    return full
 
 
 def with_halo(cells, sides, width):
@@ -60,7 +76,7 @@
         bordered = with_halo(current_tracer_values, (("grp", 1), ("tile", 0)), 1)
         padded = jnp.pad(bordered, ((0, 0), (0, 0), (1, 1)))
         current_tracer_values = advance(padded, misfit, east_speed, north_speed, wet_cells)
-    pencil = lax.all_to_all(current_tracer_values, "tile", split_axis=2, concat_axis=0, tiled=True)
+    pencil = pairwise_exchange(current_tracer_values, "tile", 2, 0)
     smoothed_field = smooth_levels(vertical_filter_matrix, pencil)
     surface_layer = smoothed_field[0]
     filtered_thermal_sensitivity = lax.all_to_all(

time: 218 us -> 185 us (0.85)
  blocking collectives: 59.5 us -> 0 us
  starting transfers between devices: 26.2 us -> 59 us
  local copies, waits for them, and re-layouts: 32.9 us -> 9.15 us
  waiting for transfers between devices: 71.9 us -> 95.6 us
  other arithmetic: 22.6 us -> 17.3 us
    all_to_all x1 -> x0, blocking collectives: 59.5 us -> none  [body(): lax.all_to_all(current_tracer_values, 'tile', split_axis=2, concat_axis=0...]
    ppermute x0 -> x7, waiting for transfers between devices: none -> 24.2 us  [pairwise_exchange(): part = lax.ppermute(part, axis, [(d, d ^ mask) for d in range(ways)])]
    ppermute x0 -> x7, starting transfers between devices: none -> 22.7 us  [pairwise_exchange(): part = lax.ppermute(part, axis, [(d, d ^ mask) for d in range(ways)])]
    unnamed x18, local copies, waits for them, and re-layouts: 13.5 us -> 0.06 us
    all_to_all x1, starting transfers between devices: 4.49 us -> 14.6 us  [body(): lax.all_to_all(smoothed_field, 'tile', split_axis=0, concat_axis=2, tiled...]
    all_to_all x1 -> x0, other arithmetic: 7.22 us -> none  [body(): lax.all_to_all(current_tracer_values, 'tile', split_axis=2, concat_axis=0...]
    all_to_all x2 -> x0, local copies, waits for them, and re-layouts: 7.09 us -> none  [body(): lax.all_to_all(current_tracer_values, 'tile', split_axis=2, concat_axis=0...]
    mul x1 -> x0, local copies, waits for them, and re-layouts: 4.74 us -> none  [advance(): wet_cells * (center + misfit + change + 0.1 * lateral + 0.15 * vertical)]
  transfers between devices with their start and end apart: 9 -> 16, of which waited for: 7 -> 10; matrix products, arithmetic and copies ran while one was open for 0% -> 1% of each run, Pallas kernels for 0% -> 0%
where the time goes in v1:
time: 185 us; the launch traced here: 184 us
  waiting for transfers between devices  95.6 us (52%)
  starting transfers between devices  59 us (32%)
  other arithmetic  17.3 us (9%)
  local copies, waits for them, and re-layouts  9.15 us (5%)
  matrix products  2.01 us (1%)
    all_to_all x1, waiting for transfers between devices, body(): lax.all_to_all(smoothed_field, 'tile', split_axis=0, concat_axis=2, tiled...  46.3 us
    ppermute x7, waiting for transfers between devices, pairwise_exchange(): part = lax.ppermute(part, axis, [(d, d ^ mask) for d in range(ways)])  24.2 us
    ppermute x7, starting transfers between devices, pairwise_exchange(): part = lax.ppermute(part, axis, [(d, d ^ mask) for d in range(ways)])  22.7 us
    ppermute x4, starting transfers between devices, with_halo(): lax.ppermute(tail, axis, [(i, (i + 1) % count) for i in range(ends)])  16.1 us
    ppermute x4, waiting for transfers between devices, with_halo(): lax.ppermute(head, axis, [((i + 1) % count, i) for i in range(ends)])  15.5 us
    all_to_all x1, starting transfers between devices, body(): lax.all_to_all(smoothed_field, 'tile', split_axis=0, concat_axis=2, tiled...  14.6 us
    ppermute x4, waiting for transfers between devices, with_halo(): lax.ppermute(tail, axis, [(i, (i + 1) % count) for i in range(ends)])  9.57 us
    mul x2, other arithmetic, advance(): wet_cells * (center + misfit + change + 0.1 * lateral + 0.15 * vertical)  8.52 us
  transfers between devices with their start and end apart: 16, of which 10 were waited for; matrix products, arithmetic and copies ran while one was open for 1% of the time, Pallas kernels for 0%

profile of v1, /device:TPU:0, one launch (start us, length us, event | category | flops | bytes accessed | tf_op | source)
XLA Modules:
  0.0 184.1 jit_solution(6232462803269719294)
XLA Ops:
  0.7 1.4 fusion.13
  2.1 2.4 %collective-permute-start = (f32[8,1,2048]{2,1,0:T(1,128)S(1)}, f32[8,1,2048]{2,1,0:T(1,128)S(1)}, u32[]{:S(2)}, u32[]{:S(2)}) collective-permute-start(f32[8,1,2048]{2,1,0:T(1,128)S(1)} %get-tuple-element.16), channel_id=1, source_target_pairs={{0,8},{8,16},{16,24},{1,9},{9,17},{17,25},{2,10},{10,18},{18,26},{... | collective-permute-start | bytes 196616 | tf_op jit(solution)/shard_map/ppermute | solution.py:33
  4.5 1.3 collective-permute-start.1
  5.8 4.0 %collective-permute-done.1 = f32[8,1,2048]{2,1,0:T(1,128)S(1)} collective-permute-done((f32[8,1,2048]{2,1,0:T(1,128)S(1)}, f32[8,1,2048]{2,1,0:T(1,128)S(1)}, u32[]{:S(2)}, u32[]{:S(2)}) %collective-permute-start.1) | collective-permute-done | bytes 65568 | tf_op jit(solution)/shard_map/ppermute | solution.py:35
  10.9 3.4 %collective-permute-start.2 = (f32[1,34,2048]{2,1,0:T(8,128)S(1)}, f32[1,34,2048]{2,1,0:T(8,128)S(1)}, u32[]{:S(2)}, u32[]{:S(2)}) collective-permute-start(f32[1,34,2048]{2,1,0:T(8,128)S(1)} %get-tuple-element.4), channel_id=1, source_target_pairs={{0,1},{1,2},{2,3},{3,4},{4,5},{5,6},{6,7},{8,9},{9,10},{10,11},{11... | collective-permute-start | bytes 835592 | tf_op jit(solution)/shard_map/ppermute | solution.py:33
  14.3 1.6 collective-permute-start.3
  15.9 4.3 %collective-permute-done.2 = f32[1,34,2048]{2,1,0:T(8,128)S(1)} collective-permute-done((f32[1,34,2048]{2,1,0:T(8,128)S(1)}, f32[1,34,2048]{2,1,0:T(8,128)S(1)}, u32[]{:S(2)}, u32[]{:S(2)}) %collective-permute-start.2) | collective-permute-done | bytes 278560 | tf_op jit(solution)/shard_map/ppermute | solution.py:33
  20.2 5.0 %collective-permute-done.3 = f32[1,34,2048]{2,1,0:T(8,128)S(1)} collective-permute-done((f32[1,34,2048]{2,1,0:T(8,128)S(1)}, f32[1,34,2048]{2,1,0:T(8,128)S(1)}, u32[]{:S(2)}, u32[]{:S(2)}) %collective-permute-start.3) | collective-permute-done | bytes 278560 | tf_op jit(solution)/shard_map/ppermute | solution.py:35
  25.2 3.1 %select_maximum_fusion.4 = f32[10,34,2050]{2,1,0:T(8,128)S(1)} fusion(f32[1,34,2048]{2,1,0:T(8,128)S(1)} %collective-permute-done.3, f32[1,34,2048]{2,1,0:T(8,128)S(1)} %collective-permute-done.2, f32[8,1,2048]{2,1,0:T(1,128)S(1)} %collective-permute-done.1, f32[8,32,2048]{2,1,0:T(8,128)S(1)} %copy-done.1, f32[8,1,2048]{2,1,0:T(1,128)S(1)} %collective-permute-done), kind=kLoop, calls=%fused_computation.6 | loop fusion | flops 8364000 | bytes 5573280 | tf_op jit(solution)/shard_map/concatenate | solution.py:31
  28.3 4.3 %fusion.10 = f32[8,32,2048]{2,1,0:T(8,128)S(1)} fusion(f32[1,34,2048]{2,1,0:T(8,128)S(1)} %collective-permute-done.3, f32[8,1,2048]{2,1,0:T(1,128)S(1)} %collective-permute-done.1, f32[8,32,2048]{2,1,0:T(8,128)S(1)} %copy-done.1, f32[8,1,2048]{2,1,0:T(1,128)S(1)} %collective-permute-done, f32[1,34,2048]{2,1,0:T(8,128)S(1)} %collective-permute-done.2, ...), kind=kLoop, calls=%fused_computation.29 | loop fusion | flops 16252928 | bytes 17465344 | tf_op jit(solution)/shard_map/mul | solution.py:55
  32.7 6.2 %collective-permute-start.4 = (f32[8,1,2048]{2,1,0:T(1,128)S(1)}, f32[8,1,2048]{2,1,0:T(1,128)S(1)}, u32[]{:S(2)}, u32[]{:S(2)}) collective-permute-start(f32[8,1,2048]{2,1,0:T(1,128)S(1)} %get-tuple-element.14), channel_id=1, source_target_pairs={{0,8},{8,16},{16,24},{1,9},{9,17},{17,25},{2,10},{10,18},{18,26},{... | collective-permute-start | bytes 196616 | tf_op jit(solution)/shard_map/ppermute | solution.py:33
  40.3 1.8 collective-permute-done.5
  42.9 4.1 %collective-permute-start.6 = (f32[1,34,2048]{2,1,0:T(8,128)}, f32[1,34,2048]{2,1,0:T(8,128)S(1)}, u32[]{:S(2)}, u32[]{:S(2)}) collective-permute-start(f32[1,34,2048]{2,1,0:T(8,128)} %get-tuple-element.2), channel_id=1, source_target_pairs={{0,1},{1,2},{2,3},{3,4},{4,5},{5,6},{6,7},{8,9},{9,10},{10,11},{11... | collective-permute-start | bytes 835592 | tf_op jit(solution)/shard_map/ppermute | solution.py:33
  47.0 1.5 collective-permute-start.7
  48.6 5.3 %collective-permute-done.6 = f32[1,34,2048]{2,1,0:T(8,128)S(1)} collective-permute-done((f32[1,34,2048]{2,1,0:T(8,128)}, f32[1,34,2048]{2,1,0:T(8,128)S(1)}, u32[]{:S(2)}, u32[]{:S(2)}) %collective-permute-start.6) | collective-permute-done | bytes 278560 | tf_op jit(solution)/shard_map/ppermute | solution.py:33
  53.8 4.7 %collective-permute-done.7 = f32[1,34,2048]{2,1,0:T(8,128)S(1)} collective-permute-done((f32[1,34,2048]{2,1,0:T(8,128)S(1)}, f32[1,34,2048]{2,1,0:T(8,128)S(1)}, u32[]{:S(2)}, u32[]{:S(2)}) %collective-permute-start.7) | collective-permute-done | bytes 278560 | tf_op jit(solution)/shard_map/ppermute | solution.py:35
  58.5 3.1 %select_maximum_fusion = f32[10,34,2050]{2,1,0:T(8,128)S(1)} fusion(f32[1,34,2048]{2,1,0:T(8,128)S(1)} %collective-permute-done.7, f32[1,34,2048]{2,1,0:T(8,128)S(1)} %collective-permute-done.6, f32[8,1,2048]{2,1,0:T(1,128)S(1)} %collective-permute-done.5, f32[8,32,2048]{2,1,0:T(8,128)S(1)} %fusion.10, f32[8,1,2048]{2,1,0:T(1,128)S(1)} %collective-permute-done.4), kind=kLoop, calls=%fused_computation.2 | loop fusion | flops 8364000 | bytes 5573280 | tf_op jit(solution)/shard_map/concatenate | solution.py:31
  61.7 4.3 %fusion.5 = f32[8,32,2048]{2,1,0:T(8,128)S(1)} fusion(f32[1,34,2048]{2,1,0:T(8,128)S(1)} %collective-permute-done.7, f32[8,1,2048]{2,1,0:T(1,128)S(1)} %collective-permute-done.5, f32[8,32,2048]{2,1,0:T(8,128)S(1)} %fusion.10, f32[8,1,2048]{2,1,0:T(1,128)S(1)} %collective-permute-done.4, f32[1,34,2048]{2,1,0:T(8,128)S(1)} %collective-permute-done.6, ...), kind=kLoop, calls=%fused_computation.16 | loop fusion | flops 16252928 | bytes 17465344 | tf_op jit(solution)/shard_map/mul | solution.py:55
  66.2 4.8 %collective-permute-start.8 = (f32[8,32,256]{2,1,0:T(8,128)S(1)}, f32[8,32,256]{2,1,0:T(8,128)S(1)}, u32[]{:S(2)}, u32[]{:S(2)}) collective-permute-start(f32[8,32,256]{2,1,0:T(8,128)S(1)} %get-tuple-element.12), channel_id=1, source_target_pairs={{0,1},{1,0},{2,3},{3,2},{4,5},{5,4},{6,7},{7,6},{8,9},{9,8},{10,11... | collective-permute-start | bytes 786440 | tf_op jit(solution)/shard_map/ppermute | solution.py:20
  71.0 3.6 %collective-permute-start.9 = (f32[8,32,256]{2,1,0:T(8,128)S(1)}, f32[8,32,256]{2,1,0:T(8,128)S(1)}, u32[]{:S(2)}, u32[]{:S(2)}) collective-permute-start(f32[8,32,256]{2,1,0:T(8,128)S(1)} %get-tuple-element.11), channel_id=1, source_target_pairs={{0,2},{1,3},{2,0},{3,1},{4,6},{5,7},{6,4},{7,5},{8,10},{9,11},{10,... | collective-permute-start | bytes 786440 | tf_op jit(solution)/shard_map/ppermute | solution.py:20
  74.6 1.3 collective-permute-start.10
  76.0 3.0 %collective-permute-start.11 = (f32[8,32,256]{2,1,0:T(8,128)S(1)}, f32[8,32,256]{2,1,0:T(8,128)S(1)}, u32[]{:S(2)}, u32[]{:S(2)}) collective-permute-start(f32[8,32,256]{2,1,0:T(8,128)S(1)} %get-tuple-element.9), channel_id=1, source_target_pairs={{0,4},{1,5},{2,6},{3,7},{4,0},{5,1},{6,2},{7,3},{8,12},{9,13},{10,... | collective-permute-start | bytes 786440 | tf_op jit(solution)/shard_map/ppermute | solution.py:20
  79.4 5.4 %collective-permute-start.13 = (f32[8,32,256]{2,1,0:T(8,128)S(1)}, f32[8,32,256]{2,1,0:T(8,128)S(1)}, u32[]{:S(2)}, u32[]{:S(2)}) collective-permute-start(f32[8,32,256]{2,1,0:T(8,128)S(1)} %get-tuple-element.7), channel_id=1, source_target_pairs={{0,6},{1,7},{2,4},{3,5},{4,2},{5,3},{6,0},{7,1},{8,14},{9,15},{10,... | collective-permute-start | bytes 786440 | tf_op jit(solution)/shard_map/ppermute | solution.py:20
  85.0 6.6 %collective-permute-done.9 = f32[8,32,256]{2,1,0:T(8,128)S(1)} collective-permute-done((f32[8,32,256]{2,1,0:T(8,128)S(1)}, f32[8,32,256]{2,1,0:T(8,128)S(1)}, u32[]{:S(2)}, u32[]{:S(2)}) %collective-permute-start.9) | collective-permute-done | bytes 262176 | tf_op jit(solution)/shard_map/ppermute | solution.py:20
  91.6 4.4 %collective-permute-start.14 = (f32[8,32,256]{2,1,0:T(8,128)S(1)}, f32[8,32,256]{2,1,0:T(8,128)S(1)}, u32[]{:S(2)}, u32[]{:S(2)}) collective-permute-start(f32[8,32,256]{2,1,0:T(8,128)S(1)} %get-tuple-element.6), channel_id=1, source_target_pairs={{0,7},{1,6},{2,5},{3,4},{4,3},{5,2},{6,1},{7,0},{8,15},{9,14},{10,... | collective-permute-start | bytes 786440 | tf_op jit(solution)/shard_map/ppermute | solution.py:20
  96.2 2.1 %collective-permute-done.10 = f32[8,32,256]{2,1,0:T(8,128)S(1)} collective-permute-done((f32[8,32,256]{2,1,0:T(8,128)S(1)}, f32[8,32,256]{2,1,0:T(8,128)S(1)}, u32[]{:S(2)}, u32[]{:S(2)}) %collective-permute-start.10) | collective-permute-done | bytes 262176 | tf_op jit(solution)/shard_map/ppermute | solution.py:20
  98.7 15.5 %collective-permute-done.12 = f32[8,32,256]{2,1,0:T(8,128)S(1)} collective-permute-done((f32[8,32,256]{2,1,0:T(8,128)S(1)}, f32[8,32,256]{2,1,0:T(8,128)S(1)}, u32[]{:S(2)}, u32[]{:S(2)}) %collective-permute-start.12) | collective-permute-done | bytes 262176 | tf_op jit(solution)/shard_map/ppermute | solution.py:20
  114.8 2.0 %convolution_bitcast_fusion = f32[64,32,256]{2,0,1:T(8,128)S(1)} fusion(f32[64,32,256]{2,0,1:T(8,128)S(1)} %copy_dynamic-update-slice_fusion, f32[64,64]{1,0:T(8,128)S(1)} %copy-done), kind=kOutput, calls=%fused_computation.37 | convolution fusion | flops 402653184 | bytes 4210688 | tf_op jit(solution)/shard_map/cz,zne->cne/dot_general | solution.py:59
  116.8 2.5 %copy.26 = f32[64,32,256]{2,1,0:T(8,128)} copy(f32[64,32,256]{2,0,1:T(8,128)S(1)} %convolution_bitcast_fusion) | data formatting | bytes 4194304 | tf_op jit(solution)/shard_map/cz,zne->cne/dot_general | solution.py:59
  119.3 14.6 %all-to-all-start = ((f32[64,32,256]{2,1,0:T(8,128)}), f32[64,32,256]{2,1,0:T(8,128)}, u32[]{:S(2)}, u32[]{:S(2)}) async-start(f32[64,32,256]{2,1,0:T(8,128)} %copy.26), calls=%async_computation | async-start | bytes 4194304 | tf_op jit(solution)/shard_map/all_to_all | solution.py:82
  134.6 46.3 %all-to-all-done = f32[64,32,256]{2,1,0:T(8,128)} async-done(((f32[64,32,256]{2,1,0:T(8,128)}), f32[64,32,256]{2,1,0:T(8,128)}, u32[]{:S(2)}, u32[]{:S(2)}) %all-to-all-start) | async-done | bytes 2097184 | tf_op jit(solution)/shard_map/all_to_all | solution.py:82
  180.9 3.2 %copy.29 = f32[8,8,4,8,256]{4,3,0,2,1:T(8,128)} copy(f32[8,8,4,8,256]{4,3,2,1,0:T(8,128)} %bitcast.6) | data formatting | bytes 4194304 | tf_op jit(solution)/shard_map/all_to_all | solution.py:82
  (41 shorter events, 5.8 us)
Async XLA Ops:
  0.6 114.1 %copy-start = (f32[64,64]{1,0:T(8,128)S(1)}, f32[64,64]{1,0:T(8,128)}, u32[]{:S(2)}) copy-start(f32[64,64]{1,0:T(8,128)} %param.13) | copy-start | bytes 49156
  0.6 24.6 %copy-start.1 = (f32[8,32,2048]{2,1,0:T(8,128)S(1)}, f32[8,32,2048]{2,1,0:T(8,128)}, u32[]{:S(2)}) copy-start(f32[8,32,2048]{2,1,0:T(8,128)} %param.7) | copy-start | bytes 6291460
  2.1 3.7 %collective-permute-start = (f32[8,1,2048]{2,1,0:T(1,128)S(1)}, f32[8,1,2048]{2,1,0:T(1,128)S(1)}, u32[]{:S(2)}, u32[]{:S(2)}) collective-permute-start(f32[8,1,2048]{2,1,0:T(1,128)S(1)} %get-tuple-element.16), channel_id=1, source_target_pairs={{0,8},{8,16},{16,24},{1,9},{9,17},{17,25},{2,10},{10,18},{18,26},{... | collective-permute-start | bytes 196616 | tf_op jit(solution)/shard_map/ppermute | solution.py:33
  4.5 5.3 %collective-permute-start.1 = (f32[8,1,2048]{2,1,0:T(1,128)S(1)}, f32[8,1,2048]{2,1,0:T(1,128)S(1)}, u32[]{:S(2)}, u32[]{:S(2)}) collective-permute-start(f32[8,1,2048]{2,1,0:T(1,128)S(1)} %get-tuple-element.17), channel_id=1, source_target_pairs={{8,0},{16,8},{24,16},{9,1},{17,9},{25,17},{10,2},{18,10},{26,18},{... | collective-permute-start | bytes 196616 | tf_op jit(solution)/shard_map/ppermute | solution.py:35
  10.9 9.3 %collective-permute-start.2 = (f32[1,34,2048]{2,1,0:T(8,128)S(1)}, f32[1,34,2048]{2,1,0:T(8,128)S(1)}, u32[]{:S(2)}, u32[]{:S(2)}) collective-permute-start(f32[1,34,2048]{2,1,0:T(8,128)S(1)} %get-tuple-element.4), channel_id=1, source_target_pairs={{0,1},{1,2},{2,3},{3,4},{4,5},{5,6},{6,7},{8,9},{9,10},{10,11},{11... | collective-permute-start | bytes 835592 | tf_op jit(solution)/shard_map/ppermute | solution.py:33
  14.3 14.0 %copy-start.2 = (f32[8,32,2048]{2,1,0:T(8,128)S(1)}, f32[8,32,2048]{2,1,0:T(8,128)}, u32[]{:S(2)}) copy-start(f32[8,32,2048]{2,1,0:T(8,128)} %param.8) | copy-start | bytes 6291460
  14.3 14.0 %copy-start.4 = (s32[8,32,2048]{2,1,0:T(8,128)S(1)}, s32[8,32,2048]{2,1,0:T(8,128)}, u32[]{:S(2)}) copy-start(s32[8,32,2048]{2,1,0:T(8,128)} %param.11) | copy-start | bytes 6291460
  14.3 14.0 %copy-start.6 = (f32[8,32,2048]{2,1,0:T(8,128)S(1)}, f32[8,32,2048]{2,1,0:T(8,128)}, u32[]{:S(2)}) copy-start(f32[8,32,2048]{2,1,0:T(8,128)} %param.10) | copy-start | bytes 6291460
  14.3 10.9 %collective-permute-start.3 = (f32[1,34,2048]{2,1,0:T(8,128)S(1)}, f32[1,34,2048]{2,1,0:T(8,128)S(1)}, u32[]{:S(2)}, u32[]{:S(2)}) collective-permute-start(f32[1,34,2048]{2,1,0:T(8,128)S(1)} %get-tuple-element.5), channel_id=1, source_target_pairs={{1,0},{2,1},{3,2},{4,3},{5,4},{6,5},{7,6},{9,8},{10,9},{11,10},{12... | collective-permute-start | bytes 835592 | tf_op jit(solution)/shard_map/ppermute | solution.py:35
  32.7 7.5 %collective-permute-start.4 = (f32[8,1,2048]{2,1,0:T(1,128)S(1)}, f32[8,1,2048]{2,1,0:T(1,128)S(1)}, u32[]{:S(2)}, u32[]{:S(2)}) collective-permute-start(f32[8,1,2048]{2,1,0:T(1,128)S(1)} %get-tuple-element.14), channel_id=1, source_target_pairs={{0,8},{8,16},{16,24},{1,9},{9,17},{17,25},{2,10},{10,18},{18,26},{... | collective-permute-start | bytes 196616 | tf_op jit(solution)/shard_map/ppermute | solution.py:33
  38.9 3.1 %collective-permute-start.5 = (f32[8,1,2048]{2,1,0:T(1,128)S(1)}, f32[8,1,2048]{2,1,0:T(1,128)S(1)}, u32[]{:S(2)}, u32[]{:S(2)}) collective-permute-start(f32[8,1,2048]{2,1,0:T(1,128)S(1)} %get-tuple-element.15), channel_id=1, source_target_pairs={{8,0},{16,8},{24,16},{9,1},{17,9},{25,17},{10,2},{18,10},{26,18},{... | collective-permute-start | bytes 196616 | tf_op jit(solution)/shard_map/ppermute | solution.py:35
  42.9 10.9 %collective-permute-start.6 = (f32[1,34,2048]{2,1,0:T(8,128)}, f32[1,34,2048]{2,1,0:T(8,128)S(1)}, u32[]{:S(2)}, u32[]{:S(2)}) collective-permute-start(f32[1,34,2048]{2,1,0:T(8,128)} %get-tuple-element.2), channel_id=1, source_target_pairs={{0,1},{1,2},{2,3},{3,4},{4,5},{5,6},{6,7},{8,9},{9,10},{10,11},{11... | collective-permute-start | bytes 835592 | tf_op jit(solution)/shard_map/ppermute | solution.py:33
  47.0 11.5 %collective-permute-start.7 = (f32[1,34,2048]{2,1,0:T(8,128)S(1)}, f32[1,34,2048]{2,1,0:T(8,128)S(1)}, u32[]{:S(2)}, u32[]{:S(2)}) collective-permute-start(f32[1,34,2048]{2,1,0:T(8,128)S(1)} %get-tuple-element.3), channel_id=1, source_target_pairs={{1,0},{2,1},{3,2},{4,3},{5,4},{6,5},{7,6},{9,8},{10,9},{11,10},{12... | collective-permute-start | bytes 835592 | tf_op jit(solution)/shard_map/ppermute | solution.py:35
  48.5 13.2 %copy-start.3 = (f32[8,32,2048]{2,1,0:T(8,128)S(1)}, f32[8,32,2048]{2,1,0:T(8,128)}, u32[]{:S(2)}) copy-start(f32[8,32,2048]{2,1,0:T(8,128)} %param.8) | copy-start | bytes 6291460
  48.5 13.2 %copy-start.5 = (s32[8,32,2048]{2,1,0:T(8,128)S(1)}, s32[8,32,2048]{2,1,0:T(8,128)}, u32[]{:S(2)}) copy-start(s32[8,32,2048]{2,1,0:T(8,128)} %param.11) | copy-start | bytes 6291460
  48.5 13.2 %copy-start.7 = (f32[8,32,2048]{2,1,0:T(8,128)S(1)}, f32[8,32,2048]{2,1,0:T(8,128)}, u32[]{:S(2)}) copy-start(f32[8,32,2048]{2,1,0:T(8,128)} %param.10) | copy-start | bytes 6291460
  66.2 13.2 %collective-permute-start.8 = (f32[8,32,256]{2,1,0:T(8,128)S(1)}, f32[8,32,256]{2,1,0:T(8,128)S(1)}, u32[]{:S(2)}, u32[]{:S(2)}) collective-permute-start(f32[8,32,256]{2,1,0:T(8,128)S(1)} %get-tuple-element.12), channel_id=1, source_target_pairs={{0,1},{1,0},{2,3},{3,2},{4,5},{5,4},{6,7},{7,6},{8,9},{9,8},{10,11... | collective-permute-start | bytes 786440 | tf_op jit(solution)/shard_map/ppermute | solution.py:20
  71.0 20.6 %collective-permute-start.9 = (f32[8,32,256]{2,1,0:T(8,128)S(1)}, f32[8,32,256]{2,1,0:T(8,128)S(1)}, u32[]{:S(2)}, u32[]{:S(2)}) collective-permute-start(f32[8,32,256]{2,1,0:T(8,128)S(1)} %get-tuple-element.11), channel_id=1, source_target_pairs={{0,2},{1,3},{2,0},{3,1},{4,6},{5,7},{6,4},{7,5},{8,10},{9,11},{10,... | collective-permute-start | bytes 786440 | tf_op jit(solution)/shard_map/ppermute | solution.py:20
  74.6 23.7 %collective-permute-start.10 = (f32[8,32,256]{2,1,0:T(8,128)S(1)}, f32[8,32,256]{2,1,0:T(8,128)S(1)}, u32[]{:S(2)}, u32[]{:S(2)}) collective-permute-start(f32[8,32,256]{2,1,0:T(8,128)S(1)} %get-tuple-element.10), channel_id=1, source_target_pairs={{0,3},{1,2},{2,1},{3,0},{4,7},{5,6},{6,5},{7,4},{8,11},{9,10},{10,... | collective-permute-start | bytes 786440 | tf_op jit(solution)/shard_map/ppermute | solution.py:20
  76.0 22.5 %collective-permute-start.11 = (f32[8,32,256]{2,1,0:T(8,128)S(1)}, f32[8,32,256]{2,1,0:T(8,128)S(1)}, u32[]{:S(2)}, u32[]{:S(2)}) collective-permute-start(f32[8,32,256]{2,1,0:T(8,128)S(1)} %get-tuple-element.9), channel_id=1, source_target_pairs={{0,4},{1,5},{2,6},{3,7},{4,0},{5,1},{6,2},{7,3},{8,12},{9,13},{10,... | collective-permute-start | bytes 786440 | tf_op jit(solution)/shard_map/ppermute | solution.py:20
  79.0 35.2 %collective-permute-start.12 = (f32[8,32,256]{2,1,0:T(8,128)S(1)}, f32[8,32,256]{2,1,0:T(8,128)S(1)}, u32[]{:S(2)}, u32[]{:S(2)}) collective-permute-start(f32[8,32,256]{2,1,0:T(8,128)S(1)} %get-tuple-element.8), channel_id=1, source_target_pairs={{0,5},{1,4},{2,7},{3,6},{4,1},{5,0},{6,3},{7,2},{8,13},{9,12},{10,... | collective-permute-start | bytes 786440 | tf_op jit(solution)/shard_map/ppermute | solution.py:20
  79.4 34.9 %collective-permute-start.13 = (f32[8,32,256]{2,1,0:T(8,128)S(1)}, f32[8,32,256]{2,1,0:T(8,128)S(1)}, u32[]{:S(2)}, u32[]{:S(2)}) collective-permute-start(f32[8,32,256]{2,1,0:T(8,128)S(1)} %get-tuple-element.7), channel_id=1, source_target_pairs={{0,6},{1,7},{2,4},{3,5},{4,2},{5,3},{6,0},{7,1},{8,14},{9,15},{10,... | collective-permute-start | bytes 786440 | tf_op jit(solution)/shard_map/ppermute | solution.py:20
  91.6 22.9 %collective-permute-start.14 = (f32[8,32,256]{2,1,0:T(8,128)S(1)}, f32[8,32,256]{2,1,0:T(8,128)S(1)}, u32[]{:S(2)}, u32[]{:S(2)}) collective-permute-start(f32[8,32,256]{2,1,0:T(8,128)S(1)} %get-tuple-element.6), channel_id=1, source_target_pairs={{0,7},{1,6},{2,5},{3,4},{4,3},{5,2},{6,1},{7,0},{8,15},{9,14},{10,... | collective-permute-start | bytes 786440 | tf_op jit(solution)/shard_map/ppermute | solution.py:20
  119.3 14.6 %copy-start.8 = (s32[32,256]{1,0:T(8,128)S(1)}, s32[32,256]{1,0:T(8,128)}, u32[]{:S(2)}) copy-start(s32[32,256]{1,0:T(8,128)} %param.12) | copy-start | bytes 98308
  119.3 61.5 %all-to-all-start = ((f32[64,32,256]{2,1,0:T(8,128)}), f32[64,32,256]{2,1,0:T(8,128)}, u32[]{:S(2)}, u32[]{:S(2)}) async-start(f32[64,32,256]{2,1,0:T(8,128)} %copy.26), calls=%async_computation | async-start | bytes 4194304 | tf_op jit(solution)/shard_map/all_to_all | solution.py:82
